TPU v7x, 1024 devices: a whole 8x8x8 slice. The times are simulated.
1024 devices in a mesh: replica: 64 (over y_hi, x, core), tensor: 16 (over z, y_lo).
Axes of the slice: x: 8, y: 8 (y_hi: 4, y_lo: 2; y = y_hi * 2 + y_lo), z: 8, core: 2. Of those that a mesh axis runs over, the one named last changes fastest.
Arguments:
- hidden_rows: bfloat16 [512, 8, 8192], P('replica'), may hold values from -6 to 6
- prior_bias: bfloat16 [2048], P('tensor'), may hold values from -4 to 4
- cache_blocks: bfloat16 [16, 256, 1024, 256], P('tensor', 'replica'), may hold values from -5 to 5
- queries: bfloat16 [16, 256, 8, 1024], P('tensor', 'replica'), may hold values from -125 to 125
- cache_lengths: int32 [512], P('replica'), may hold values from 2 to 1024, as said below
- updated_rows: bfloat16 [8192, 2048], P(('replica', 'tensor')), may hold values from -0.0625 to 0.0625
Outputs:
- attended: bfloat16 [16, 256, 8, 1024], P('tensor', 'replica')
- updated_columns: bfloat16 [8192, 2048], P(None, 'tensor')
Inputs may be any that keep to these rules, and one draw needn't show every extreme that they name: `cache_lengths`: each row's length lies between 2 and 1024; some row has exactly 1024.
All inputs are finite; a program needn't handle non-finite values.
Results may differ from a plain program's by a relative error of at most 0.0065.
Values may be sent and summed in bfloat16 or wider, within the bound.
A program may use at most 32 MiB of HBM per device.

v0:
```python
import math

import jax
import jax.numpy as jnp
from jax import lax
from jax.sharding import PartitionSpec as P

rope_base = 1000000.0


def from_partner(shard, axis, apart):
    return lax.ppermute(shard, axis, [(i, i ^ 1 << apart) for i in range(lax.axis_size(axis))])


def rotate_keys(vectors, positions):
    extent = vectors.shape[-1]
    middle = extent // 2
    frequency = jnp.exp(
        jnp.arange(middle, dtype=jnp.float32) * (-2.0 * math.log(rope_base) / extent)
    )
    angles = positions.astype(jnp.float32)[..., None] * frequency
    cos_part = jnp.concatenate([jnp.cos(angles), jnp.cos(angles)], axis=-1)
    sine_part = jnp.concatenate([jnp.sin(angles), jnp.sin(angles)], axis=-1)
    turned = jnp.concatenate([-vectors[..., middle:], vectors[..., :middle]], axis=-1)
    return vectors * cos_part + turned * sine_part


def attend(query_rows, cache_rows, new_keys, new_values, row_lengths):
    row_count, step_count, query_width = query_rows.shape
    extent = new_keys.shape[-1]
    groups = query_width // extent
    query_heads = query_rows.reshape(row_count, step_count, groups, extent)
    cached_keys = cache_rows[:, :, :extent]
    cached_values = cache_rows[:, :, extent:]
    score_scale = 1.0 / math.sqrt(extent)
    old_scores = (
        jnp.einsum("rsgd,rpd->rsgp", query_heads, cached_keys, preferred_element_type=jnp.float32)
        * score_scale
    )
    fresh_scores = (
        jnp.einsum("rsgd,rud->rsgu", query_heads, new_keys, preferred_element_type=jnp.float32)
        * score_scale
    )
    places = jnp.arange(cache_rows.shape[1], dtype=jnp.int32)
    old_valid = places[None, :] < row_lengths[:, None]
    old_scores = jnp.where(old_valid[:, None, None, :], old_scores, -1e30)
    steps_range = jnp.arange(step_count, dtype=jnp.int32)
    causal = steps_range[None, :] <= steps_range[:, None]
    fresh_scores = jnp.where(causal[None, :, None, :], fresh_scores, -1e30)
    peak_score = jnp.maximum(jnp.max(old_scores, axis=-1), jnp.max(fresh_scores, axis=-1))[
        ..., None
    ]
    old_exp = jnp.exp(old_scores - peak_score)
    fresh_exp = jnp.exp(fresh_scores - peak_score)
    denominator = jnp.sum(old_exp, axis=-1, keepdims=True) + jnp.sum(
        fresh_exp, axis=-1, keepdims=True
    )
    old_weights = (old_exp / denominator).astype(jnp.bfloat16)
    fresh_weights = (fresh_exp / denominator).astype(jnp.bfloat16)
    output = jnp.einsum(
        "rsgp,rpd->rsgd", old_weights, cached_values, preferred_element_type=jnp.float32
    )
    output = output + jnp.einsum(
        "rsgu,rud->rsgd", fresh_weights, new_values, preferred_element_type=jnp.float32
    )
    return output.reshape(row_count, step_count, query_width).astype(jnp.bfloat16)


def per_device(hidden_rows, prior_bias, cache_blocks, queries, cache_lengths, updated_rows):
    tensor_count = lax.axis_size("tensor")
    replica_count = lax.axis_size("replica")
    block_rows = updated_rows.shape[0]
    collected = lax.all_gather(updated_rows, "replica", axis=0, tiled=True)
    sorted_rows = lax.all_to_all(collected, "tensor", split_axis=1, concat_axis=0, tiled=True)
    column_width = sorted_rows.shape[1]
    arranged = sorted_rows.reshape(tensor_count, replica_count, block_rows, column_width)
    arranged = jnp.transpose(arranged, (1, 0, 2, 3))
    updated_columns = arranged.reshape(replica_count * tensor_count * block_rows, column_width)
    position = lax.axis_index("tensor")
    parity = position % 2
    row_count, step_count, model_width = hidden_rows.shape
    flattened = hidden_rows.reshape(row_count * step_count, model_width)
    projected = jnp.dot(flattened, updated_columns, preferred_element_type=jnp.float32)
    projected = (projected + prior_bias.astype(jnp.float32)).reshape(row_count, step_count, -1)
    positions = cache_lengths[:, None] + jnp.arange(step_count, dtype=jnp.int32)[None, :]
    rotated = rotate_keys(projected, positions)
    column_part = jnp.where(parity == 0, rotated, projected).astype(jnp.bfloat16)
    paired = column_part.reshape(2, row_count // 2, step_count, -1)
    own_part = lax.dynamic_index_in_dim(paired, parity, 0, keepdims=False)
    sent_part = lax.dynamic_index_in_dim(paired, 1 - parity, 0, keepdims=False)
    partner = from_partner(sent_part, "tensor", 0)
    new_keys = jnp.where(parity == 0, own_part, partner)
    new_values = jnp.where(parity == 0, partner, own_part)
    own_lengths = lax.dynamic_index_in_dim(
        cache_lengths.reshape(2, row_count // 2), parity, 0, keepdims=False
    )
    attended = attend(queries[0], cache_blocks[0], new_keys, new_values, own_lengths)[None]
    return (attended, updated_columns)


def solution(mesh):
    placed = (
        P("replica", None, None),
        P("tensor"),
        P("tensor", "replica", None, None),
        P("tensor", "replica", None, None),
        P("replica"),
        P(("replica", "tensor"), None),
    )
    return jax.shard_map(
        per_device,
        mesh=mesh,
        in_specs=placed,
        out_specs=(P("tensor", "replica", None, None), P(None, "tensor")),
        check_vma=False,
    )
```

profile of v0, /device:TPU:1, one launch (start us, length us, event | category | flops | bytes accessed | tf_op | source)
XLA Modules:
  0.0 194.6 jit_solution(1842046188416193572)
XLA Ops:
  7.2 0.0 copy-start
  7.2 0.0 all-gather.2.cloned.1.call-start
  7.2 0.7 all-gather.2.cloned.1.call-update
  7.9 107.0 %all-gather.2.cloned.1.call-done = bf16[512,2048]{1,0:T(8,128)(2,1)} async-done(((bf16[8,2048]{1,0:T(8,128)(2,1)}), bf16[512,2048]{1,0:T(8,128)(2,1)}) %all-gather.2.cloned.1.call-update) | async-done | bytes 2097168 | tf_op jit(solution)/shard_map/all_gather | solution.py:73
  114.9 3.9 %copy.21 = bf16[512,2048]{0,1:T(8,128)(2,1)} copy(bf16[512,2048]{1,0:T(8,128)(2,1)} %all-gather.2.cloned.1.call-done) | data formatting | bytes 4194304 | tf_op jit(solution)/shard_map/all_gather | solution.py:73
  118.9 8.1 %all-to-all-start = ((bf16[512,16,128]{0,2,1:T(8,128)(2,1)}), bf16[512,16,128]{0,2,1:T(8,128)(2,1)S(1)}, u32[]{:S(2)}, u32[]{:S(2)}) async-start(bf16[512,16,128]{0,2,1:T(8,128)(2,1)} %bitcast.62), calls=%async_computation | async-start | bytes 4194304 | tf_op jit(solution)/shard_map/all_to_all | solution.py:74
  127.0 0.0 copy-done.5
  127.0 0.0 copy-done.6
  127.0 0.1 reshape.124
  127.1 0.1 iota_compare_fusion
  127.2 0.1 add_convert_fusion
  127.3 0.2 multiply_sine_fusion
  127.5 0.0 copy-done.4
  127.5 2.7 %fusion.26 = (f32[4,8,8]{2,1,0:T(8,128)S(1)}, f32[4,8,8,1024]{3,2,1,0:T(8,128)}) fusion(bf16[4,1024,256]{2,1,0:T(8,128)(2,1)} %bitcast.68, bf16[4,8,8,128]{3,1,2,0:T(8,128)(2,1)S(1)} %bitcast.70, pred[4,1024]{1,0:T(4,128)(4,1)S(1)} %iota_compare_fusion), kind=kOutput, calls=%fused_computation.49 | convolution fusion | flops 67895040 | bytes 2167808 | tf_op jit(solution)/shard_map/rsgd,rpd->rsgp/dot_general | solution.py:37
  130.2 45.5 %all-to-all-done = bf16[512,16,128]{0,2,1:T(8,128)(2,1)S(1)} async-done(((bf16[512,16,128]{0,2,1:T(8,128)(2,1)}), bf16[512,16,128]{0,2,1:T(8,128)(2,1)S(1)}, u32[]{:S(2)}, u32[]{:S(2)}) %all-to-all-start) | async-done | bytes 2097184 | tf_op jit(solution)/shard_map/all_to_all | solution.py:74
  175.6 2.4 %copy.22 = bf16[16,512,128]{2,1,0:T(8,128)(2,1)} copy(bf16[16,512,128]{1,2,0:T(8,128)(2,1)S(1)} %bitcast.61) | data formatting | bytes 4194304 | tf_op jit(solution)/shard_map/all_to_all | solution.py:74
  178.0 2.2 %copy.23 = bf16[64,16,8,128]{3,2,1,0:T(8,128)(2,1)S(1)} copy(bf16[64,16,8,128]{3,2,0,1:T(8,128)(2,1)} %bitcast.65) | data formatting | bytes 4194304 | tf_op jit(solution)/shard_map/transpose | solution.py:77
  180.2 0.0 copy-start.1
  180.2 0.0 copy-start.2
  180.2 0.0 copy-done
  180.2 0.0 copy-start.3
  180.2 0.5 convolution_add_fusion.1
  180.7 0.1 slice_negate_fusion
  180.8 0.1 fusion.16
  180.9 2.3 %collective-permute-start = (bf16[4,8,128]{2,1,0:T(8,128)(2,1)S(1)}, bf16[4,8,128]{2,1,0:T(8,128)(2,1)S(1)}, u32[]{:S(2)}, u32[]{:S(2)}) collective-permute-start(bf16[4,8,128]{2,1,0:T(8,128)(2,1)S(1)} %dynamic-slice_bitcast_fusion), channel_id=1, source_target_pairs={{0,1},{1,0},{2,3},{3,2},{4,5},{5,4},{6,7},{7,6},{8,9},{9,8},{10,11... | collective-permute-start | bytes 24584 | tf_op jit(solution)/shard_map/ppermute | solution.py:12
  183.3 2.3 %collective-permute-done = bf16[4,8,128]{2,1,0:T(8,128)(2,1)S(1)} collective-permute-done((bf16[4,8,128]{2,1,0:T(8,128)(2,1)S(1)}, bf16[4,8,128]{2,1,0:T(8,128)(2,1)S(1)}, u32[]{:S(2)}, u32[]{:S(2)}) %collective-permute-start) | collective-permute-done | bytes 8224 | tf_op jit(solution)/shard_map/ppermute | solution.py:12
  185.6 0.4 fusion.27
  186.0 0.1 fusion.9
  186.1 0.3 fusion.6
  186.4 0.4 fusion.4
  186.8 0.2 fusion.3
  187.1 0.7 convert_element_type.40
  (13 shorter events, 0.1 us)
Async XLA Ops:
  7.2 173.0 %copy-start = (bf16[8,8,8192]{2,1,0:T(8,128)(2,1)S(1)}, bf16[8,8,8192]{2,1,0:T(8,128)(2,1)}, u32[]{:S(2)}) copy-start(bf16[8,8,8192]{2,1,0:T(8,128)(2,1)} %param.6) | copy-start | bytes 3145732
  7.2 107.8 %all-gather.2.cloned.1.call-start = ((), (), s32[]{:S(2)}) async-start(), calls=%async_computation.1 | async-start | bytes 2129920 | tf_op jit(solution)/shard_map/all_gather | solution.py:73
  118.9 8.1 %copy-start.5 = (bf16[128]{0:T(256)(128)(2,1)S(1)}, bf16[128]{0:T(256)(128)(2,1)}, u32[]{:S(2)}) copy-start(bf16[128]{0:T(256)(128)(2,1)} %param.7) | copy-start | bytes 772
  118.9 8.1 %copy-start.6 = (s32[8]{0:T(128)S(1)}, s32[8]{0:T(128)}, u32[]{:S(2)}) copy-start(s32[8]{0:T(128)} %param.10) | copy-start | bytes 100
  118.9 8.6 %copy-start.4 = (bf16[1,4,8,1024]{3,2,1,0:T(8,128)(2,1)S(1)}, bf16[1,4,8,1024]{3,2,1,0:T(8,128)(2,1)}, u32[]{:S(2)}) copy-start(bf16[1,4,8,1024]{3,2,1,0:T(8,128)(2,1)} %param.9) | copy-start | bytes 196612
  118.9 56.8 %all-to-all-start = ((bf16[512,16,128]{0,2,1:T(8,128)(2,1)}), bf16[512,16,128]{0,2,1:T(8,128)(2,1)S(1)}, u32[]{:S(2)}, u32[]{:S(2)}) async-start(bf16[512,16,128]{0,2,1:T(8,128)(2,1)} %bitcast.62), calls=%async_computation | async-start | bytes 4194304 | tf_op jit(solution)/shard_map/all_to_all | solution.py:74
  180.2 6.2 %copy-start.1 = (bf16[64,16,8,128]{3,2,1,0:T(8,128)(2,1)}, bf16[64,16,8,128]{3,2,1,0:T(8,128)(2,1)S(1)}, u32[]{:S(2)}) copy-start(bf16[64,16,8,128]{3,2,1,0:T(8,128)(2,1)S(1)} %copy.23) | copy-start | bytes 6291460
  180.2 5.9 %copy-start.2 = (f32[4,8,8,1024]{3,2,1,0:T(8,128)S(1)}, f32[4,8,8,1024]{3,2,1,0:T(8,128)}, u32[]{:S(2)}) copy-start(f32[4,8,8,1024]{3,2,1,0:T(8,128)} %get-tuple-element.7) | copy-start | bytes 3145732
  180.2 6.2 %copy-start.3 = (bf16[1,4,1024,256]{3,2,1,0:T(8,128)(2,1)S(1)}, bf16[1,4,1024,256]{3,2,1,0:T(8,128)(2,1)}, u32[]{:S(2)}) copy-start(bf16[1,4,1024,256]{3,2,1,0:T(8,128)(2,1)} %param.8) | copy-start | bytes 6291460
  180.9 4.7 %collective-permute-start = (bf16[4,8,128]{2,1,0:T(8,128)(2,1)S(1)}, bf16[4,8,128]{2,1,0:T(8,128)(2,1)S(1)}, u32[]{:S(2)}, u32[]{:S(2)}) collective-permute-start(bf16[4,8,128]{2,1,0:T(8,128)(2,1)S(1)} %dynamic-slice_bitcast_fusion), channel_id=1, source_target_pairs={{0,1},{1,0},{2,3},{3,2},{4,5},{5,4},{6,7},{7,6},{8,9},{9,8},{10,11... | collective-permute-start | bytes 24584 | tf_op jit(solution)/shard_map/ppermute | solution.py:12
Sparse Core Ops, SparseCore 0:
  12.5 102.3 all-gather.1
where the time goes:
time: 197 us; the launch traced here: 195 us
  waiting for transfers between devices  155 us (79%)
  between operations  14.2 us (7%)
  starting transfers between devices  10.5 us (5%)
  local copies, waits for them, and re-layouts  9.25 us (5%)
  matrix products  4.21 us (2%)
    all_gather x1, waiting for transfers between devices, per_device(): collected = lax.all_gather(updated_rows, 'replica', axis=0, tiled=True)  107 us
    all_to_all x1, waiting for transfers between devices, per_device(): lax.all_to_all(collected, 'tensor', split_axis=1, concat_axis=0, tiled=True)  45.5 us
    all_to_all x1, starting transfers between devices, per_device(): lax.all_to_all(collected, 'tensor', split_axis=1, concat_axis=0, tiled=True)  8.08 us
  transfers between devices with their start and end apart: 3, of which 3 were waited for; matrix products, arithmetic and copies ran while one was open for 2% of the time, Pallas kernels for 0%

commit v1 on v0

v1 whole, which is shorter than its diff:
```python
import functools
import math

import jax
import jax.numpy as jnp
from jax import lax
from jax.experimental import pallas as pl
from jax.experimental.pallas import tpu as pltpu
from jax.sharding import PartitionSpec as P

ROPE_BASE = 1000000.0
HD = 128
NEG = -1e30
MESH = pl.DeviceIdType.MESH
NT = (((1,), (1,)), ((), ()))


def kernel(
    NY, NX, NTEN, PIECE, STEPS,
    rows_hbm, hidden_hbm, cache_hbm, query_hbm, bias_ref, len_ref,
    cols, att,
    parts, hidden, cache, query, mine, other,
    part_send, part_recv, send, recv, load, pair_send, pair_recv,
):
    rep = lax.axis_index("replica")
    ten = lax.axis_index("tensor")
    core = lax.rem(rep, 2)
    chip = lax.div(rep, 2)
    x = lax.rem(chip, NX)
    y = lax.div(chip, NX)
    parity = lax.rem(ten, 2)
    block = NTEN * PIECE

    def replica(dy, dx, c=None):
        yy = lax.rem(y + dy + 2 * NY, NY)
        xx = lax.rem(x + dx + 2 * NX, NX)
        return (yy * NX + xx) * 2 + (core if c is None else c)

    right, left = replica(0, 1), replica(0, -1)
    sibling = replica(0, 0, 1 - core)
    ahead = [replica(d, 0) for d in range(1, NY)]
    peers = [lax.rem(ten + k, NTEN) for k in range(1, NTEN)]

    barrier = pltpu.get_barrier_semaphore()
    for p in peers:
        pl.semaphore_signal(barrier, inc=1, device_id=(rep, p), device_id_type=MESH)
    for r in [right, left, sibling, *ahead]:
        pl.semaphore_signal(barrier, inc=1, device_id=(r, ten), device_id_type=MESH)

    loads = [
        pltpu.make_async_copy(query_hbm, query, load.at[0]),
        pltpu.make_async_copy(cache_hbm, cache, load.at[1]),
        pltpu.make_async_copy(hidden_hbm, hidden, load.at[2]),
        pltpu.make_async_copy(
            rows_hbm.at[:, pl.ds(pl.multiple_of(ten * HD, HD), HD)], parts.at[0], load.at[3]
        ),
    ]
    loads[3].start()
    for c in loads[:3]:
        c.start()
    pl.semaphore_wait(barrier, len(peers) + 3 + len(ahead))

    for k, p in enumerate(peers, 1):
        pltpu.make_async_remote_copy(
            src_ref=rows_hbm.at[:, pl.ds(pl.multiple_of(p * HD, HD), HD)],
            dst_ref=parts.at[k],
            send_sem=part_send,
            recv_sem=part_recv,
            device_id=(rep, p),
            device_id_type=MESH,
        ).start()

    def at(r):
        return cols.at[pl.ds(pl.multiple_of(r * block, block), block), :]

    def push(r, to):
        pltpu.make_async_remote_copy(
            src_ref=at(r), dst_ref=at(r), send_sem=send, recv_sem=recv.at[r],
            device_id=(to, ten), device_id_type=MESH,
        ).start()

    def arrived(r):
        pltpu.make_async_copy(at(r), at(r), recv.at[r]).wait()

    lane = lax.broadcasted_iota(jnp.int32, (1, HD), 1)
    half = lax.rem(lane, HD // 2).astype(jnp.float32)
    frequency = jnp.exp(half * (-2.0 * math.log(ROPE_BASE) / HD))
    step = lax.broadcasted_iota(jnp.int32, (STEPS, HD), 0)
    n_rows = hidden.shape[0] // STEPS
    position = jnp.concatenate([step + len_ref[b] for b in range(n_rows)], axis=0)
    angle = position.astype(jnp.float32) * frequency
    cosine = jnp.cos(angle)
    sine = jnp.sin(angle) * jnp.where(lane < HD // 2, -1.0, 1.0)

    scale = 1.0 / math.sqrt(HD)
    n_att = query.shape[0]
    groups = query.shape[2] // HD
    queries, peaks, totals, sums = [], [], [], []

    def attend_cached(i):
        if i == 0:
            loads[0].wait()
            loads[1].wait()
        wide = query[i].astype(jnp.float32)
        q = jnp.concatenate([wide[:, g * HD : (g + 1) * HD] for g in range(groups)], axis=0)
        q = q.astype(jnp.bfloat16)
        s = lax.dot_general(q, cache[i, :, :HD], NT, preferred_element_type=jnp.float32) * scale
        place = lax.broadcasted_iota(jnp.int32, s.shape, 1)
        s = jnp.where(place < len_ref[parity * n_att + i], s, NEG)
        m = jnp.max(s, axis=1, keepdims=True)
        e = jnp.exp(s - m)
        queries.append(q)
        peaks.append(m)
        totals.append(jnp.sum(e, axis=1, keepdims=True))
        sums.append(
            jnp.dot(e.astype(jnp.bfloat16), cache[i, :, HD:], preferred_element_type=jnp.float32)
        )

    projected = [jnp.zeros((hidden.shape[0], HD), jnp.float32)]

    def project(dy, dx):
        c = lax.div(replica(dy, dx), 2)
        span = pl.ds(pl.multiple_of(c * 2 * block, 2 * block), 2 * block)
        projected[0] += jnp.dot(hidden[:, span], cols[span, :], preferred_element_type=jnp.float32)

    attend_cached(0)

    loads[3].wait()
    pltpu.make_async_copy(parts.at[pl.ds(1, NTEN - 1)], parts.at[pl.ds(1, NTEN - 1)], part_recv).wait()
    pieces = [
        parts[lax.rem(ten - k + NTEN, NTEN)].astype(jnp.float32) for k in range(NTEN)
    ]
    cols[pl.ds(pl.multiple_of(rep * block, block), block), :] = jnp.concatenate(
        pieces, axis=0
    ).astype(jnp.bfloat16)

    push(rep, right)
    push(rep, left)
    for r in ahead:
        push(rep, r)
    push(rep, sibling)

    attend_cached(1)
    order = [d for d in (1, NY - 1, 2) if d < NY] if NY > 2 else list(range(1, NY))
    for d in order:
        r = replica(d, 0)
        arrived(r)
        push(r, right)
        push(r, left)
        push(r, sibling)

    waiting = [(d, 0) for d in [0, *order]]
    cached_left = list(range(2, n_att))
    loads[2].wait()
    for s in range(1, NX // 2 + 1):
        fresh = []
        for j, d in enumerate([0, *order]):
            to_right = NX // 2 if j % 2 == 0 else NX // 2 - 1
            to_left = NX - 1 - to_right
            if s <= to_right:
                r = replica(d, -s)
                arrived(r)
                if s < to_right:
                    push(r, right)
                push(r, sibling)
                fresh.append((d, -s))
            if s <= to_left:
                r = replica(d, s)
                arrived(r)
                if s < to_left:
                    push(r, left)
                push(r, sibling)
                fresh.append((d, s))
        if cached_left:
            attend_cached(cached_left.pop(0))
        for dy, dx in waiting:
            arrived(replica(dy, dx, 1 - core))
            project(dy, dx)
        waiting = fresh
    for i in cached_left:
        attend_cached(i)
    for dy, dx in waiting:
        arrived(replica(dy, dx, 1 - core))
        project(dy, dx)

    whole = projected[0] + bias_ref[...].astype(jnp.float32)
    rotated = whole * cosine + pltpu.roll(whole, HD // 2, 1) * sine
    whole = jnp.where(parity == 0, rotated, whole).astype(jnp.bfloat16)
    n_half = whole.shape[0] // 2
    mine[0] = whole[:n_half]
    mine[1] = whole[n_half:]
    exchange = pltpu.make_async_remote_copy(
        src_ref=mine.at[1 - parity], dst_ref=other, send_sem=pair_send, recv_sem=pair_recv,
        device_id=(rep, ten + 1 - 2 * parity), device_id_type=MESH,
    )
    exchange.start()
    exchange.wait()
    kept, got = mine[parity], other[...]
    new_keys = jnp.where(parity == 0, kept, got)
    new_values = jnp.where(parity == 0, got, kept)

    q = jnp.concatenate(queries, axis=0)
    s = lax.dot_general(q, new_keys, NT, preferred_element_type=jnp.float32) * scale
    of_query = lax.broadcasted_iota(jnp.int32, s.shape, 0)
    of_key = lax.broadcasted_iota(jnp.int32, s.shape, 1)
    same_row = lax.div(of_query, groups * STEPS) == lax.div(of_key, STEPS)
    causal = lax.rem(of_key, STEPS) <= lax.rem(of_query, STEPS)
    s = jnp.where(same_row & causal, s, NEG)
    old_peak = jnp.concatenate(peaks, axis=0)
    peak = jnp.maximum(old_peak, jnp.max(s, axis=1, keepdims=True))
    e = jnp.exp(s - peak)
    shrink = jnp.exp(old_peak - peak)
    total = jnp.concatenate(totals, axis=0) * shrink + jnp.sum(e, axis=1, keepdims=True)
    out = jnp.concatenate(sums, axis=0) * shrink
    out += jnp.dot(e.astype(jnp.bfloat16), new_values, preferred_element_type=jnp.float32)
    out = out / total
    for i in range(n_att):
        base = i * groups * STEPS
        att[i] = jnp.concatenate(
            [out[base + g * STEPS : base + (g + 1) * STEPS] for g in range(groups)], axis=1
        ).astype(jnp.bfloat16)

    pltpu.make_async_copy(
        parts.at[pl.ds(1, NTEN - 1)], parts.at[pl.ds(1, NTEN - 1)], part_send
    ).wait()
    sent = cols.at[pl.ds(0, (2 * NY * NX - 1) * block), :]
    pltpu.make_async_copy(sent, sent, send).wait()


def solution(mesh):
    n_rep, n_ten = mesh.shape["replica"], mesh.shape["tensor"]
    NX = 8
    NY = n_rep // (2 * NX)

    def per_device(hidden_rows, prior_bias, cache_blocks, queries, cache_lengths, updated_rows):
        n_rows, steps, width = hidden_rows.shape
        piece = updated_rows.shape[0]
        any_space = pl.BlockSpec(memory_space=pl.ANY)
        vmem = pl.BlockSpec(memory_space=pltpu.VMEM)
        block = n_ten * piece
        attended, columns = pl.pallas_call(
            functools.partial(kernel, NY, NX, n_ten, piece, steps),
            out_shape=(
                jax.ShapeDtypeStruct((n_rep * block, HD), jnp.bfloat16),
                jax.ShapeDtypeStruct(queries.shape[1:], jnp.bfloat16),
            ),
            in_specs=[any_space] * 4 + [vmem, pl.BlockSpec(memory_space=pltpu.SMEM)],
            out_specs=(vmem, vmem),
            scratch_shapes=[
                pltpu.VMEM((n_ten, piece, HD), jnp.bfloat16),
                pltpu.VMEM((n_rows * steps, width), jnp.bfloat16),
                pltpu.VMEM(cache_blocks.shape[1:], jnp.bfloat16),
                pltpu.VMEM(queries.shape[1:], jnp.bfloat16),
                pltpu.VMEM((2, n_rows * steps // 2, HD), jnp.bfloat16),
                pltpu.VMEM((n_rows * steps // 2, HD), jnp.bfloat16),
                pltpu.SemaphoreType.DMA,
                pltpu.SemaphoreType.DMA,
                pltpu.SemaphoreType.DMA,
                pltpu.SemaphoreType.DMA((n_rep,)),
                pltpu.SemaphoreType.DMA((4,)),
                pltpu.SemaphoreType.DMA,
                pltpu.SemaphoreType.DMA,
            ],
            compiler_params=pltpu.CompilerParams(
                collective_id=0, has_side_effects=True, vmem_limit_bytes=40 << 20
            ),
        )(
            updated_rows,
            hidden_rows.reshape(n_rows * steps, width),
            cache_blocks[0],
            queries[0],
            prior_bias.reshape(1, HD),
            cache_lengths,
        )[::-1]
        return attended[None], columns

    return jax.shard_map(
        per_device,
        mesh=mesh,
        in_specs=(
            P("replica", None, None),
            P("tensor"),
            P("tensor", "replica", None, None),
            P("tensor", "replica", None, None),
            P("replica"),
            P(("replica", "tensor"), None),
        ),
        out_specs=(P("tensor", "replica", None, None), P(None, "tensor")),
        check_vma=False,
    )
```

time: 197 us -> 60 us (0.30); the launches traced: 195 us -> 59.6 us
  waiting for transfers between devices: 155 us -> 0 us
  Pallas kernels: 0 us -> 51.3 us
  between operations: 14.2 us -> 0.65 us
  starting transfers between devices: 10.5 us -> 0 us
  matrix products: 4.21 us -> 0 us
    all_gather x1 -> x0, waiting for transfers between devices: 107 us -> none  [per_device(): collected = lax.all_gather(updated_rows, 'replica', axis=0, tiled=True)]
    pallas_call x0 -> x1, Pallas kernels: none -> 51.3 us  [per_device(): pl.pallas_call(functools.partial(kernel, NY, NX, n_ten, piece, steps), ou...]
    all_to_all x1 -> x0, waiting for transfers between devices: 45.5 us -> none  [per_device(): lax.all_to_all(collected, 'tensor', split_axis=1, concat_axis=0, tiled=True)]
    all_to_all x1 -> x0, starting transfers between devices: 8.08 us -> none  [per_device(): lax.all_to_all(collected, 'tensor', split_axis=1, concat_axis=0, tiled=True)]
    unnamed x14, local copies, waits for them, and re-layouts: 0.04 us -> 7.66 us
    dot_general x5 -> x0, matrix products: 4.21 us -> none  [the longest x1 2.68 us: attend(): jnp.einsum('rsgd,rpd->rsgp', query_heads, cached_keys, preferred_element_...]
    all_gather x1 -> x0, local copies, waits for them, and re-layouts: 3.92 us -> none  [per_device(): collected = lax.all_gather(updated_rows, 'replica', axis=0, tiled=True)]
    all_to_all x1 -> x0, local copies, waits for them, and re-layouts: 2.36 us -> none  [per_device(): lax.all_to_all(collected, 'tensor', split_axis=1, concat_axis=0, tiled=True)]
  transfers between devices with their start and end apart: 3 -> 0, of which waited for: 3 -> 0; matrix products, arithmetic and copies ran while one was open for 2% -> 0% of each run, Pallas kernels for 0% -> 0%
where the time goes in v1:
time: 60 us; the launch traced here: 59.6 us
  Pallas kernels  51.3 us (86%)
  local copies, waits for them, and re-layouts  7.66 us (13%)
  between operations  0.65 us (1%)
    pallas_call x1, Pallas kernels, per_device(): pl.pallas_call(functools.partial(kernel, NY, NX, n_ten, piece, steps), ou...  51.3 us
    unnamed x14, local copies, waits for them, and re-layouts  7.66 us

profile of v1, /device:TPU:1, one launch (start us, length us, event | category | flops | bytes accessed | tf_op | source)
XLA Modules:
  0.0 59.6 jit_solution(3634344540023681976)
XLA Ops:
  0.6 0.0 copy-start
  0.6 1.6 %copy-done = bf16[1,4,1024,256]{3,2,1,0:T(8,128)(2,1)S(1)} copy-done((bf16[1,4,1024,256]{3,2,1,0:T(8,128)(2,1)S(1)}, bf16[1,4,1024,256]{3,2,1,0:T(8,128)(2,1)}, u32[]{:S(2)}) %copy-start) | copy-done | bytes 2097176
  2.2 0.0 copy-start.1
  2.2 1.2 %copy-done.1 = bf16[8,8,8192]{2,1,0:T(8,128)(2,1)S(1)} copy-done((bf16[8,8,8192]{2,1,0:T(8,128)(2,1)S(1)}, bf16[8,8,8192]{2,1,0:T(8,128)(2,1)}, u32[]{:S(2)}) %copy-start.1) | copy-done | bytes 1048600
  3.4 0.0 copy-start.2
  3.5 0.8 %copy-done.2 = bf16[1,4,8,1024]{3,2,1,0:T(8,128)(2,1)S(1)} copy-done((bf16[1,4,8,1024]{3,2,1,0:T(8,128)(2,1)S(1)}, bf16[1,4,8,1024]{3,2,1,0:T(8,128)(2,1)}, u32[]{:S(2)}) %copy-start.2) | copy-done | bytes 65560
  4.3 0.0 copy-start.3
  4.3 0.8 %copy-done.3 = bf16[8,2048]{1,0:T(8,128)(2,1)S(1)} copy-done((bf16[8,2048]{1,0:T(8,128)(2,1)S(1)}, bf16[8,2048]{1,0:T(8,128)(2,1)}, u32[]{:S(2)}) %copy-start.3) | copy-done | bytes 32792
  5.0 0.0 copy-start.4
  5.0 0.7 %copy-done.4 = bf16[128]{0:T(256)(128)(2,1)S(1)} copy-done((bf16[128]{0:T(256)(128)(2,1)S(1)}, bf16[128]{0:T(256)(128)(2,1)}, u32[]{:S(2)}) %copy-start.4) | copy-done | bytes 280
  5.7 0.0 copy-start.5
  5.7 0.7 %copy-done.5 = s32[8]{0:T(128)S(1)} copy-done((s32[8]{0:T(128)S(1)}, s32[8]{0:T(128)}, u32[]{:S(2)}) %copy-start.5) | copy-done | bytes 56
  6.4 51.3 %shard_map.77 = (bf16[8192,128]{1,0:T(8,128)(2,1)S(1)}, bf16[4,8,1024]{2,1,0:T(8,128)(2,1)S(1)}) custom-call(bf16[8,2048]{1,0:T(8,128)(2,1)S(1)} %copy-done.3, bf16[64,8192]{1,0:T(8,128)(2,1)S(1)} %bitcast.6, bf16[4,1024,256]{2,1,0:T(8,128)(2,1)S(1)} %bitcast.5, bf16[4,8,1024]{2,1,0:T(8,128)(2,1)S(1)} %bitcast.7, bf16[1,128]{1,0:T(2,128)(2,1)S(1)} %bitcast.9, ...), custom_call_target="tpu_custom_call" | custom-call | tf_op jit(solution)/shard_map/pallas_call | solution.py:241
  57.7 0.6 %copy.10 = bf16[1,4,8,1024]{3,2,1,0:T(8,128)(2,1)} copy(bf16[1,4,8,1024]{3,2,1,0:T(8,128)(2,1)S(1)} %bitcast.8) | data formatting | bytes 131072
  58.3 1.3 %copy.11 = bf16[8192,128]{1,0:T(8,128)(2,1)} copy(bf16[8192,128]{1,0:T(8,128)(2,1)S(1)} %get-tuple-element.9) | data formatting | bytes 4194304
Async XLA Ops:
  0.6 1.6 %copy-start = (bf16[1,4,1024,256]{3,2,1,0:T(8,128)(2,1)S(1)}, bf16[1,4,1024,256]{3,2,1,0:T(8,128)(2,1)}, u32[]{:S(2)}) copy-start(bf16[1,4,1024,256]{3,2,1,0:T(8,128)(2,1)} %param.8) | copy-start | bytes 6291460
  2.2 1.2 %copy-start.1 = (bf16[8,8,8192]{2,1,0:T(8,128)(2,1)S(1)}, bf16[8,8,8192]{2,1,0:T(8,128)(2,1)}, u32[]{:S(2)}) copy-start(bf16[8,8,8192]{2,1,0:T(8,128)(2,1)} %param.6) | copy-start | bytes 3145732
  3.4 0.8 %copy-start.2 = (bf16[1,4,8,1024]{3,2,1,0:T(8,128)(2,1)S(1)}, bf16[1,4,8,1024]{3,2,1,0:T(8,128)(2,1)}, u32[]{:S(2)}) copy-start(bf16[1,4,8,1024]{3,2,1,0:T(8,128)(2,1)} %param.9) | copy-start | bytes 196612
  4.3 0.8 %copy-start.3 = (bf16[8,2048]{1,0:T(8,128)(2,1)S(1)}, bf16[8,2048]{1,0:T(8,128)(2,1)}, u32[]{:S(2)}) copy-start(bf16[8,2048]{1,0:T(8,128)(2,1)} %rows_hbm.1) | copy-start | bytes 98308
  5.0 0.7 %copy-start.4 = (bf16[128]{0:T(256)(128)(2,1)S(1)}, bf16[128]{0:T(256)(128)(2,1)}, u32[]{:S(2)}) copy-start(bf16[128]{0:T(256)(128)(2,1)} %param.7) | copy-start | bytes 772
  5.7 0.7 %copy-start.5 = (s32[8]{0:T(128)S(1)}, s32[8]{0:T(128)}, u32[]{:S(2)}) copy-start(s32[8]{0:T(128)} %len_ref.1) | copy-start | bytes 100

commit v2 on v1

--- a/solution.py
+++ b/solution.py
@@ -17,9 +17,9 @@
 
 def kernel(
     NY, NX, NTEN, PIECE, STEPS,
-    rows_hbm, hidden_hbm, cache_hbm, query_hbm, bias_ref, len_ref,
+    rows_hbm, hidden_hbm, cache_hbm, query_hbm, bias_hbm, len_hbm,
     cols, att,
-    parts, hidden, cache, query, mine, other,
+    parts, hidden, cache, query, bias_ref, len_ref, mine, other,
     part_send, part_recv, send, recv, load, pair_send, pair_recv,
 ):
     rep = lax.axis_index("replica")
@@ -36,15 +36,20 @@
         xx = lax.rem(x + dx + 2 * NX, NX)
         return (yy * NX + xx) * 2 + (core if c is None else c)
 
-    right, left = replica(0, 1), replica(0, -1)
     sibling = replica(0, 0, 1 - core)
+    beside = {d: replica(0, d) for d in (1, -1, 2, -2)}
     ahead = [replica(d, 0) for d in range(1, NY)]
-    peers = [lax.rem(ten + k, NTEN) for k in range(1, NTEN)]
+    layer = lax.div(ten, 2)
 
     barrier = pltpu.get_barrier_semaphore()
-    for p in peers:
-        pl.semaphore_signal(barrier, inc=1, device_id=(rep, p), device_id_type=MESH)
-    for r in [right, left, sibling, *ahead]:
+    for p in reversed(range(NTEN)):
+
+        @pl.when((p >= 2 * layer) & (p != ten))
+        def _():
+            pl.semaphore_signal(barrier, inc=1, device_id=(rep, p), device_id_type=MESH)
+
+    plane = [*beside.values(), *ahead, sibling]
+    for r in plane:
         pl.semaphore_signal(barrier, inc=1, device_id=(r, ten), device_id_type=MESH)
 
     loads = [
@@ -52,23 +57,30 @@
         pltpu.make_async_copy(cache_hbm, cache, load.at[1]),
         pltpu.make_async_copy(hidden_hbm, hidden, load.at[2]),
         pltpu.make_async_copy(
-            rows_hbm.at[:, pl.ds(pl.multiple_of(ten * HD, HD), HD)], parts.at[0], load.at[3]
+            rows_hbm.at[:, pl.ds(pl.multiple_of(ten * HD, HD), HD)], parts.at[ten], load.at[3]
         ),
+        pltpu.make_async_copy(len_hbm, len_ref, load.at[4]),
+        pltpu.make_async_copy(bias_hbm, bias_ref, load.at[5]),
     ]
-    loads[3].start()
-    for c in loads[:3]:
-        c.start()
-    pl.semaphore_wait(barrier, len(peers) + 3 + len(ahead))
-
-    for k, p in enumerate(peers, 1):
+    for i in (3, 4, 5, 0, 1, 2):
+        loads[i].start()
+    pl.semaphore_wait(barrier, len(plane) + 2 * layer + 1)
+
+    def give(p):
         pltpu.make_async_remote_copy(
-            src_ref=rows_hbm.at[:, pl.ds(pl.multiple_of(p * HD, HD), HD)],
-            dst_ref=parts.at[k],
-            send_sem=part_send,
-            recv_sem=part_recv,
-            device_id=(rep, p),
-            device_id_type=MESH,
+            src_ref=rows_hbm.at[:, pl.ds(p * HD, HD)], dst_ref=parts.at[ten],
+            send_sem=part_send, recv_sem=part_recv.at[ten],
+            device_id=(rep, p), device_id_type=MESH,
         ).start()
+
+    def take(p):
+        pltpu.make_async_copy(parts.at[p], parts.at[p], part_recv.at[p]).wait()
+
+    for p in range(NTEN):
+
+        @pl.when((p < 2 * layer + 2) & (p != ten))
+        def _():
+            give(p)
 
     def at(r):
         return cols.at[pl.ds(pl.multiple_of(r * block, block), block), :]
@@ -87,6 +99,7 @@
     frequency = jnp.exp(half * (-2.0 * math.log(ROPE_BASE) / HD))
     step = lax.broadcasted_iota(jnp.int32, (STEPS, HD), 0)
     n_rows = hidden.shape[0] // STEPS
+    loads[4].wait()
     position = jnp.concatenate([step + len_ref[b] for b in range(n_rows)], axis=0)
     angle = position.astype(jnp.float32) * frequency
     cosine = jnp.cos(angle)
@@ -123,66 +136,87 @@
         span = pl.ds(pl.multiple_of(c * 2 * block, 2 * block), 2 * block)
         projected[0] += jnp.dot(hidden[:, span], cols[span, :], preferred_element_type=jnp.float32)
 
-    attend_cached(0)
+    for i in range(n_att):
+        attend_cached(i)
+    loads[2].wait()
+
+    for p in range(2, NTEN, 2):
+
+        @pl.when(p > 2 * layer)
+        def _():
+            take(p)
+            take(p + 1)
+            give(p)
+            give(p + 1)
+
+    for p in range(NTEN):
+
+        @pl.when((p < 2 * layer + 2) & (p != ten))
+        def _():
+            take(p)
 
     loads[3].wait()
-    pltpu.make_async_copy(parts.at[pl.ds(1, NTEN - 1)], parts.at[pl.ds(1, NTEN - 1)], part_recv).wait()
-    pieces = [
-        parts[lax.rem(ten - k + NTEN, NTEN)].astype(jnp.float32) for k in range(NTEN)
-    ]
+    pieces = [parts[p].astype(jnp.float32) for p in range(NTEN)]
     cols[pl.ds(pl.multiple_of(rep * block, block), block), :] = jnp.concatenate(
         pieces, axis=0
     ).astype(jnp.bfloat16)
 
-    push(rep, right)
-    push(rep, left)
+    def spread(dy):
+        r = replica(dy, 0)
+        for d in (2, -2, 1, -1):
+            push(r, beside[d])
+        push(r, sibling)
+
+    def onward(dy, far):
+        for d in (2, -2):
+            r = replica(dy, -d)
+            arrived(r)
+            if far == d:
+                push(r, beside[d])
+            push(r, beside[d // 2])
+            push(r, sibling)
+
+    def handed(dy, d):
+        r = replica(dy, -d)
+        arrived(r)
+        push(r, sibling)
+
+    def both(dy, dx):
+        arrived(replica(dy, dx, 1 - core))
+        project(dy, dx)
+
     for r in ahead:
         push(rep, r)
-    push(rep, sibling)
-
-    attend_cached(1)
-    order = [d for d in (1, NY - 1, 2) if d < NY] if NY > 2 else list(range(1, NY))
-    for d in order:
-        r = replica(d, 0)
-        arrived(r)
-        push(r, right)
-        push(r, left)
-        push(r, sibling)
-
-    waiting = [(d, 0) for d in [0, *order]]
-    cached_left = list(range(2, n_att))
-    loads[2].wait()
-    for s in range(1, NX // 2 + 1):
-        fresh = []
-        for j, d in enumerate([0, *order]):
-            to_right = NX // 2 if j % 2 == 0 else NX // 2 - 1
-            to_left = NX - 1 - to_right
-            if s <= to_right:
-                r = replica(d, -s)
-                arrived(r)
-                if s < to_right:
-                    push(r, right)
-                push(r, sibling)
-                fresh.append((d, -s))
-            if s <= to_left:
-                r = replica(d, s)
-                arrived(r)
-                if s < to_left:
-                    push(r, left)
-                push(r, sibling)
-                fresh.append((d, s))
-        if cached_left:
-            attend_cached(cached_left.pop(0))
-        for dy, dx in waiting:
-            arrived(replica(dy, dx, 1 - core))
-            project(dy, dx)
-        waiting = fresh
-    for i in cached_left:
-        attend_cached(i)
-    for dy, dx in waiting:
-        arrived(replica(dy, dx, 1 - core))
-        project(dy, dx)
-
+    spread(0)
+    ys = [d for d in (1, NY - 1, 2)][: NY - 1]
+    fars = {d: (2, -2)[i % 2] for i, d in enumerate([0, *ys])}
+    onward(0, fars[0])
+    for d in ys:
+        arrived(replica(d, 0))
+        spread(d)
+    handed(0, 1)
+    handed(0, -1)
+    both(0, 0)
+    for dy in ys:
+        onward(dy, fars[dy])
+    for dx in (1, -1, 2, -2):
+        both(0, dx)
+    for dy in ys:
+        handed(dy, 1)
+        handed(dy, -1)
+    for dy in ys:
+        both(dy, 0)
+    for dy in [0, *ys]:
+        for d in (3, -3, 4):
+            handed(dy, d)
+        if dy != 0:
+            for dx in (1, -1, 2, -2):
+                both(dy, dx)
+    for dy in [0, *ys]:
+        for dx in (3, -3, 4):
+            both(dy, dx)
+
+    loads[5].wait()
     whole = projected[0] + bias_ref[...].astype(jnp.float32)
     rotated = whole * cosine + pltpu.roll(whole, HD // 2, 1) * sine
     whole = jnp.where(parity == 0, rotated, whole).astype(jnp.bfloat16)
@@ -220,9 +254,8 @@
             [out[base + g * STEPS : base + (g + 1) * STEPS] for g in range(groups)], axis=1
         ).astype(jnp.bfloat16)
 
-    pltpu.make_async_copy(
-        parts.at[pl.ds(1, NTEN - 1)], parts.at[pl.ds(1, NTEN - 1)], part_send
-    ).wait()
+    given = parts.at[pl.ds(0, NTEN - 1)]
+    pltpu.make_async_copy(given, given, part_send).wait()
     sent = cols.at[pl.ds(0, (2 * NY * NX - 1) * block), :]
     pltpu.make_async_copy(sent, sent, send).wait()
 
@@ -235,7 +268,6 @@
     def per_device(hidden_rows, prior_bias, cache_blocks, queries, cache_lengths, updated_rows):
         n_rows, steps, width = hidden_rows.shape
         piece = updated_rows.shape[0]
-        any_space = pl.BlockSpec(memory_space=pl.ANY)
         vmem = pl.BlockSpec(memory_space=pltpu.VMEM)
         block = n_ten * piece
         attended, columns = pl.pallas_call(
@@ -244,20 +276,22 @@
                 jax.ShapeDtypeStruct((n_rep * block, HD), jnp.bfloat16),
                 jax.ShapeDtypeStruct(queries.shape[1:], jnp.bfloat16),
             ),
-            in_specs=[any_space] * 4 + [vmem, pl.BlockSpec(memory_space=pltpu.SMEM)],
+            in_specs=[pl.BlockSpec(memory_space=pltpu.HBM)] * 6,
             out_specs=(vmem, vmem),
             scratch_shapes=[
                 pltpu.VMEM((n_ten, piece, HD), jnp.bfloat16),
                 pltpu.VMEM((n_rows * steps, width), jnp.bfloat16),
                 pltpu.VMEM(cache_blocks.shape[1:], jnp.bfloat16),
                 pltpu.VMEM(queries.shape[1:], jnp.bfloat16),
+                pltpu.VMEM((1, HD), jnp.bfloat16),
+                pltpu.SMEM((n_rows,), jnp.int32),
                 pltpu.VMEM((2, n_rows * steps // 2, HD), jnp.bfloat16),
                 pltpu.VMEM((n_rows * steps // 2, HD), jnp.bfloat16),
                 pltpu.SemaphoreType.DMA,
-                pltpu.SemaphoreType.DMA,
+                pltpu.SemaphoreType.DMA((n_ten,)),
                 pltpu.SemaphoreType.DMA,
                 pltpu.SemaphoreType.DMA((n_rep,)),
-                pltpu.SemaphoreType.DMA((4,)),
+                pltpu.SemaphoreType.DMA((6,)),
                 pltpu.SemaphoreType.DMA,
                 pltpu.SemaphoreType.DMA,
             ],
@@ -265,12 +299,17 @@
                 collective_id=0, has_side_effects=True, vmem_limit_bytes=40 << 20
             ),
         )(
-            updated_rows,
-            hidden_rows.reshape(n_rows * steps, width),
-            cache_blocks[0],
-            queries[0],
-            prior_bias.reshape(1, HD),
-            cache_lengths,
+            *(
+                pltpu.with_memory_space_constraint(a, pltpu.HBM)
+                for a in (
+                    updated_rows,
+                    hidden_rows.reshape(n_rows * steps, width),
+                    cache_blocks[0],
+                    queries[0],
+                    prior_bias.reshape(1, HD),
+                    cache_lengths,
+                )
+            )
         )[::-1]
         return attended[None], columns
 

time: 60 us -> 54.4 us (0.907)
  local copies, waits for them, and re-layouts: 7.66 us -> 1.95 us
    unnamed x14 -> x2, local copies, waits for them, and re-layouts: 7.66 us -> 1.95 us
where the time goes in v2:
time: 54.4 us; the launch traced here: 54.3 us
  Pallas kernels  51.7 us (95%)
  local copies, waits for them, and re-layouts  1.95 us (4%)
  between operations  0.64 us (1%)
    pallas_call x1, Pallas kernels, per_device(): pl.pallas_call(functools.partial(kernel, NY, NX, n_ten, piece, steps), ou...  51.7 us
    unnamed x2, local copies, waits for them, and re-layouts  1.95 us

profile of v2, /device:TPU:1, one launch (start us, length us, event | category | flops | bytes accessed | tf_op | source)
XLA Modules:
  0.0 54.3 jit_solution(15379380816329421614)
XLA Ops:
  0.6 51.7 %shard_map.77 = (bf16[8192,128]{1,0:T(8,128)(2,1)S(1)}, bf16[4,8,1024]{2,1,0:T(8,128)(2,1)S(1)}) custom-call(bf16[8,2048]{1,0:T(8,128)(2,1)} %rows_hbm.1, bf16[64,8192]{1,0:T(8,128)(2,1)} %bitcast.7, bf16[4,1024,256]{2,1,0:T(8,128)(2,1)} %bitcast.6, bf16[4,8,1024]{2,1,0:T(8,128)(2,1)} %bitcast.8, bf16[1,128]{1,0:T(2,128)(2,1)} %bitcast.9, s32[8]{0:T(128)} %len_hbm.1), custom_call_target="tpu_custom_call" | custom-call | tf_op jit(solution)/shard_map/pallas_call | solution.py:273
  52.3 0.6 %copy.10 = bf16[1,4,8,1024]{3,2,1,0:T(8,128)(2,1)} copy(bf16[1,4,8,1024]{3,2,1,0:T(8,128)(2,1)S(1)} %bitcast.5) | data formatting | bytes 131072
  53.0 1.3 %copy.11 = bf16[8192,128]{1,0:T(8,128)(2,1)} copy(bf16[8192,128]{1,0:T(8,128)(2,1)S(1)} %get-tuple-element.9) | data formatting | bytes 4194304

commit v3 on v2

--- a/solution.py
+++ b/solution.py
@@ -13,6 +13,8 @@
 NEG = -1e30
 MESH = pl.DeviceIdType.MESH
 NT = (((1,), (1,)), ((), ()))
+LATE = 6
+STAGES = ((0, 4, 2), (4, 4, 2))
 
 
 def kernel(
@@ -20,7 +22,7 @@
     rows_hbm, hidden_hbm, cache_hbm, query_hbm, bias_hbm, len_hbm,
     cols, att,
     parts, hidden, cache, query, bias_ref, len_ref, mine, other,
-    part_send, part_recv, send, recv, load, pair_send, pair_recv,
+    part_send, part_recv, send, one_y, one_x, all_y, all_x, hand, heard, load, pair_send, pair_recv,
 ):
     rep = lax.axis_index("replica")
     ten = lax.axis_index("tensor")
@@ -36,21 +38,30 @@
         xx = lax.rem(x + dx + 2 * NX, NX)
         return (yy * NX + xx) * 2 + (core if c is None else c)
 
+    def wrap(i, n):
+        return lax.rem(i + 2 * n, n)
+
     sibling = replica(0, 0, 1 - core)
-    beside = {d: replica(0, d) for d in (1, -1, 2, -2)}
-    ahead = [replica(d, 0) for d in range(1, NY)]
+    near = sorted(range(1 - NX // 2, NX // 2 + 1), key=abs)[1:]
+    ahead = sorted(range(1 - NY // 2, NY // 2 + 1), key=abs)[1:]
     layer = lax.div(ten, 2)
+    partner = ten + 1 - 2 * parity
 
     barrier = pltpu.get_barrier_semaphore()
-    for p in reversed(range(NTEN)):
-
-        @pl.when((p >= 2 * layer) & (p != ten))
+    late = layer >= LATE
+    plane = [replica(0, d) for d in near] + [replica(d, 0) for d in ahead] + [sibling]
+
+    @pl.when(jnp.logical_not(late))
+    def _():
+        for r in plane:
+            pl.semaphore_signal(barrier, inc=1, device_id=(r, ten), device_id_type=MESH)
+        pl.semaphore_signal(barrier, inc=1, device_id=(rep, partner), device_id_type=MESH)
+
+    for p in reversed(range(2, NTEN)):
+
+        @pl.when(p >= 2 * layer + 2)
         def _():
             pl.semaphore_signal(barrier, inc=1, device_id=(rep, p), device_id_type=MESH)
-
-    plane = [*beside.values(), *ahead, sibling]
-    for r in plane:
-        pl.semaphore_signal(barrier, inc=1, device_id=(r, ten), device_id_type=MESH)
 
     loads = [
         pltpu.make_async_copy(query_hbm, query, load.at[0]),
@@ -64,11 +75,17 @@
     ]
     for i in (3, 4, 5, 0, 1, 2):
         loads[i].start()
-    pl.semaphore_wait(barrier, len(plane) + 2 * layer + 1)
+    @pl.when(late)
+    def _():
+        pl.semaphore_wait(barrier, 2 * layer)
+
+    @pl.when(jnp.logical_not(late))
+    def _():
+        pl.semaphore_wait(barrier, len(plane) + 2 * layer + 1)
 
     def give(p):
         pltpu.make_async_remote_copy(
-            src_ref=rows_hbm.at[:, pl.ds(p * HD, HD)], dst_ref=parts.at[ten],
+            src_ref=rows_hbm.at[:, pl.ds(pl.multiple_of(p * HD, HD), HD)], dst_ref=parts.at[ten],
             send_sem=part_send, recv_sem=part_recv.at[ten],
             device_id=(rep, p), device_id_type=MESH,
         ).start()
@@ -76,23 +93,73 @@
     def take(p):
         pltpu.make_async_copy(parts.at[p], parts.at[p], part_recv.at[p]).wait()
 
-    for p in range(NTEN):
-
-        @pl.when((p < 2 * layer + 2) & (p != ten))
+    for p in range(NTEN - 2):
+
+        @pl.when(p < 2 * layer)
         def _():
             give(p)
 
-    def at(r):
-        return cols.at[pl.ds(pl.multiple_of(r * block, block), block), :]
-
-    def push(r, to):
+    @pl.when(jnp.logical_not(late))
+    def _():
+        give(partner)
+
+    unit = 2 * PIECE
+
+    def along_y(yy_or_all, xx, stage, c):
+        first, _, part = STAGES[stage]
+        return cols.at[yy_or_all, xx, c, pl.ds(first * unit, part * unit), :]
+
+    def along_x(yy, xx_or_all, stage, c):
+        first, n, part = STAGES[stage]
+        return cols.at[yy, xx_or_all, c, pl.ds((first + part) * unit, (n - part) * unit), :]
+
+    def push(ref, to, kind, recv_sem):
         pltpu.make_async_remote_copy(
-            src_ref=at(r), dst_ref=at(r), send_sem=send, recv_sem=recv.at[r],
+            src_ref=ref, dst_ref=ref, send_sem=send.at[kind], recv_sem=recv_sem,
             device_id=(to, ten), device_id_type=MESH,
         ).start()
 
-    def arrived(r):
-        pltpu.make_async_copy(at(r), at(r), recv.at[r]).wait()
+    def arrived(ref, recv_sem):
+        pltpu.make_async_copy(ref, ref, recv_sem).wait()
+
+    every = slice(None)
+
+    def begin(stage):
+        first, n, _ = STAGES[stage]
+        pieces = [parts[p].astype(jnp.float32) for p in range(2 * first, 2 * (first + n))]
+        cols[y, x, core, pl.ds(first * unit, n * unit), :] = jnp.concatenate(
+            pieces, axis=0
+        ).astype(jnp.bfloat16)
+        for d in reversed(ahead):
+            push(along_y(y, x, stage, core), replica(d, 0), 0, one_y.at[stage, y])
+        for d in reversed(near):
+            push(along_x(y, x, stage, core), replica(0, d), 0, one_x.at[stage, x])
+
+    def turn(stage):
+        for d in ahead:
+            yy = wrap(y - d, NY)
+            arrived(along_y(yy, x, stage, core), one_y.at[stage, yy])
+        for d in reversed(near):
+            push(along_y(every, x, stage, core), replica(0, d), 1, all_x.at[stage, x])
+        for d in near:
+            xx = wrap(x - d, NX)
+            arrived(along_x(y, xx, stage, core), one_x.at[stage, xx])
+        for d in reversed(ahead):
+            push(along_x(y, every, stage, core), replica(d, 0), 2, all_y.at[stage, y])
+
+    def finish(stage):
+        for d in ahead:
+            yy = wrap(y - d, NY)
+            arrived(along_x(yy, every, stage, core), all_y.at[stage, yy])
+        push(along_x(every, every, stage, core), sibling, 3, hand.at[stage, 1])
+        for d in near:
+            xx = wrap(x - d, NX)
+            arrived(along_y(every, xx, stage, core), all_x.at[stage, xx])
+        push(along_y(every, every, stage, core), sibling, 3, hand.at[stage, 0])
+
+    def got(stage):
+        arrived(along_x(every, every, stage, 1 - core), hand.at[stage, 1])
+        arrived(along_y(every, every, stage, 1 - core), hand.at[stage, 0])
 
     lane = lax.broadcasted_iota(jnp.int32, (1, HD), 1)
     half = lax.rem(lane, HD // 2).astype(jnp.float32)
@@ -129,95 +196,107 @@
             jnp.dot(e.astype(jnp.bfloat16), cache[i, :, HD:], preferred_element_type=jnp.float32)
         )
 
-    projected = [jnp.zeros((hidden.shape[0], HD), jnp.float32)]
-
-    def project(dy, dx):
-        c = lax.div(replica(dy, dx), 2)
-        span = pl.ds(pl.multiple_of(c * 2 * block, 2 * block), 2 * block)
-        projected[0] += jnp.dot(hidden[:, span], cols[span, :], preferred_element_type=jnp.float32)
+
+    def project(yy):
+        wide = NX * 2 * block
+        return jnp.dot(
+            hidden[:, yy * wide : (yy + 1) * wide], cols[yy].reshape(wide, HD), preferred_element_type=jnp.float32
+        )
 
     for i in range(n_att):
         attend_cached(i)
     loads[2].wait()
 
-    for p in range(2, NTEN, 2):
-
-        @pl.when(p > 2 * layer)
-        def _():
-            take(p)
-            take(p + 1)
-            give(p)
-            give(p + 1)
-
-    for p in range(NTEN):
-
-        @pl.when((p < 2 * layer + 2) & (p != ten))
-        def _():
-            take(p)
+    def answer(first, end):
+        for p in range(2 * first, 2 * end, 2):
+
+            @pl.when(p > 2 * layer)
+            def _():
+                take(p)
+                take(p + 1)
+                give(p)
+                give(p + 1)
+
+    def meet(first, end):
+        for p in range(2 * first, 2 * end, 2):
+
+            @pl.when(p < 2 * layer)
+            def _():
+                take(p)
+                take(p + 1)
+
+            if p == 0:
+
+                @pl.when(late)
+                def _():
+                    give(partner)
+
+            @pl.when(p == 2 * layer)
+            def _():
+                take(partner)
+
+    def hear(first):
+        for p in range(2 * first, NTEN, 2):
+
+            @pl.when(layer == 0)
+            def _():
+                take(p)
+                take(p + 1)
+                for r in plane:
+                    pl.semaphore_signal(
+                        heard.at[p // 2 - first], inc=1, device_id=(r, ten), device_id_type=MESH
+                    )
+
+            @pl.when(layer > 0)
+            def _():
+                take(p)
+                take(p + 1)
+                give(p)
+                give(p + 1)
+
+    def confirm(first):
+        for p in range(2 * first, NTEN, 2):
+
+            @pl.when(layer == 0)
+            def _():
+                pl.semaphore_wait(heard.at[p // 2 - first], len(plane))
+                give(p)
+                give(p + 1)
 
     loads[3].wait()
-    pieces = [parts[p].astype(jnp.float32) for p in range(NTEN)]
-    cols[pl.ds(pl.multiple_of(rep * block, block), block), :] = jnp.concatenate(
-        pieces, axis=0
-    ).astype(jnp.bfloat16)
-
-    def spread(dy):
-        r = replica(dy, 0)
-        for d in (2, -2, 1, -1):
-            push(r, beside[d])
-        push(r, sibling)
-
-    def onward(dy, far):
-        for d in (2, -2):
-            r = replica(dy, -d)
-            arrived(r)
-            if far == d:
-                push(r, beside[d])
-            push(r, beside[d // 2])
-            push(r, sibling)
-
-    def handed(dy, d):
-        r = replica(dy, -d)
-        arrived(r)
-        push(r, sibling)
-
-    def both(dy, dx):
-        arrived(replica(dy, dx, 1 - core))
-        project(dy, dx)
-
-    for r in ahead:
-        push(rep, r)
-    spread(0)
-    ys = [d for d in (1, NY - 1, 2)][: NY - 1]
-    fars = {d: (2, -2)[i % 2] for i, d in enumerate([0, *ys])}
-    onward(0, fars[0])
-    for d in ys:
-        arrived(replica(d, 0))
-        spread(d)
-    handed(0, 1)
-    handed(0, -1)
-    both(0, 0)
-    for dy in ys:
-        onward(dy, fars[dy])
-    for dx in (1, -1, 2, -2):
-        both(0, dx)
-    for dy in ys:
-        handed(dy, 1)
-        handed(dy, -1)
-    for dy in ys:
-        both(dy, 0)
-    for dy in [0, *ys]:
-        for d in (3, -3, 4):
-            handed(dy, d)
-        if dy != 0:
-            for dx in (1, -1, 2, -2):
-                both(dy, dx)
-    for dy in [0, *ys]:
-        for dx in (3, -3, 4):
-            both(dy, dx)
+
+    @pl.when(layer < 3)
+    def _():
+        answer(0, 4)
+        meet(0, 4)
+        begin(0)
+        answer(4, LATE)
+        hear(LATE)
+        begin(1)
+        turn(0)
+        confirm(LATE)
+        turn(1)
+
+    @pl.when(layer >= 3)
+    def _():
+        answer(3, 8)
+        meet(0, 4)
+        begin(0)
+        meet(4, 8)
+        begin(1)
+        turn(0)
+        turn(1)
+
+    finish(0)
+    got(0)
+    finish(1)
+    got(1)
+    projected = project(0)
+    for yy in range(1, NY):
+        projected += project(yy)
 
     loads[5].wait()
-    whole = projected[0] + bias_ref[...].astype(jnp.float32)
+    whole = projected + bias_ref[...].astype(jnp.float32)
     rotated = whole * cosine + pltpu.roll(whole, HD // 2, 1) * sine
     whole = jnp.where(parity == 0, rotated, whole).astype(jnp.bfloat16)
     n_half = whole.shape[0] // 2
@@ -225,7 +304,7 @@
     mine[1] = whole[n_half:]
     exchange = pltpu.make_async_remote_copy(
         src_ref=mine.at[1 - parity], dst_ref=other, send_sem=pair_send, recv_sem=pair_recv,
-        device_id=(rep, ten + 1 - 2 * parity), device_id_type=MESH,
+        device_id=(rep, partner), device_id_type=MESH,
     )
     exchange.start()
     exchange.wait()
@@ -256,8 +335,15 @@
 
     given = parts.at[pl.ds(0, NTEN - 1)]
     pltpu.make_async_copy(given, given, part_send).wait()
-    sent = cols.at[pl.ds(0, (2 * NY * NX - 1) * block), :]
-    pltpu.make_async_copy(sent, sent, send).wait()
+    for kind, ref in enumerate(
+        (
+            cols.at[0, pl.ds(0, (NX + NY - 2) // 2), 0],
+            cols.at[pl.ds(0, NY // 2), pl.ds(0, NX - 1), 0],
+            cols.at[pl.ds(0, NY - 1), pl.ds(0, NX // 2), 0],
+            cols.at[pl.ds(0, NY // 2)],
+        )
+    ):
+        pltpu.make_async_copy(ref, ref, send.at[kind]).wait()
 
 
 def solution(mesh):
@@ -273,7 +359,7 @@
         attended, columns = pl.pallas_call(
             functools.partial(kernel, NY, NX, n_ten, piece, steps),
             out_shape=(
-                jax.ShapeDtypeStruct((n_rep * block, HD), jnp.bfloat16),
+                jax.ShapeDtypeStruct((NY, NX, 2, block, HD), jnp.bfloat16),
                 jax.ShapeDtypeStruct(queries.shape[1:], jnp.bfloat16),
             ),
             in_specs=[pl.BlockSpec(memory_space=pltpu.HBM)] * 6,
@@ -289,8 +375,9 @@
                 pltpu.VMEM((n_rows * steps // 2, HD), jnp.bfloat16),
                 pltpu.SemaphoreType.DMA,
                 pltpu.SemaphoreType.DMA((n_ten,)),
-                pltpu.SemaphoreType.DMA,
-                pltpu.SemaphoreType.DMA((n_rep,)),
+                pltpu.SemaphoreType.DMA((4,)),
+                *[pltpu.SemaphoreType.DMA((len(STAGES), n)) for n in (NY, NX, NY, NX, 2)],
+                pltpu.SemaphoreType.REGULAR((n_ten // 2 - LATE,)),
                 pltpu.SemaphoreType.DMA((6,)),
                 pltpu.SemaphoreType.DMA,
                 pltpu.SemaphoreType.DMA,
@@ -311,7 +398,7 @@
                 )
             )
         )[::-1]
-        return attended[None], columns
+        return attended[None], columns.reshape(n_rep * block, HD)
 
     return jax.shard_map(
         per_device,

time: 54.4 us -> 48.4 us (0.89)
  Pallas kernels: 51.7 us -> 45.7 us
    pallas_call x1, Pallas kernels: 51.7 us -> 45.7 us  [per_device(): pl.pallas_call(functools.partial(kernel, NY, NX, n_ten, piece, steps), ou...]
where the time goes in v3:
time: 48.4 us; the launch traced here: 48.3 us
  Pallas kernels  45.7 us (94%)
  local copies, waits for them, and re-layouts  1.95 us (4%)
  between operations  0.64 us (1%)
    pallas_call x1, Pallas kernels, per_device(): pl.pallas_call(functools.partial(kernel, NY, NX, n_ten, piece, steps), ou...  45.7 us
    unnamed x2, local copies, waits for them, and re-layouts  1.95 us

profile of v3, /device:TPU:1, one launch (start us, length us, event | category | flops | bytes accessed | tf_op | source)
XLA Modules:
  0.0 48.3 jit_solution(3336467232249970665)
XLA Ops:
  0.6 45.7 %shard_map.77 = (bf16[4,8,2,128,128]{4,3,2,1,0:T(8,128)(2,1)S(1)}, bf16[4,8,1024]{2,1,0:T(8,128)(2,1)S(1)}) custom-call(bf16[8,2048]{1,0:T(8,128)(2,1)} %rows_hbm.1, bf16[64,8192]{1,0:T(8,128)(2,1)} %bitcast.9, bf16[4,1024,256]{2,1,0:T(8,128)(2,1)} %bitcast.8, bf16[4,8,1024]{2,1,0:T(8,128)(2,1)} %bitcast.10, bf16[1,128]{1,0:T(2,128)(2,1)} %bitcast.11, s32[8]{0:T(128)} %len_hbm.1), custom_call_target="tpu_custom_call" | custom-call | tf_op jit(solution)/shard_map/pallas_call | solution.py:359
  46.3 0.6 %copy.10 = bf16[1,4,8,1024]{3,2,1,0:T(8,128)(2,1)} copy(bf16[1,4,8,1024]{3,2,1,0:T(8,128)(2,1)S(1)} %bitcast.7) | data formatting | bytes 131072
  46.9 1.3 %copy.11 = bf16[8192,128]{1,0:T(8,128)(2,1)} copy(bf16[8192,128]{1,0:T(8,128)(2,1)S(1)} %bitcast.6) | data formatting | bytes 4194304

commit v4 on v3

--- a/solution.py
+++ b/solution.py
@@ -14,13 +14,13 @@
 MESH = pl.DeviceIdType.MESH
 NT = (((1,), (1,)), ((), ()))
 LATE = 6
-STAGES = ((0, 4, 2), (4, 4, 2))
+STAGES = ((0, 3, 2), (3, 1, 0), (4, 4, 2), (0, 4, 2), (4, 4, 2))
 
 
 def kernel(
     NY, NX, NTEN, PIECE, STEPS,
     rows_hbm, hidden_hbm, cache_hbm, query_hbm, bias_hbm, len_hbm,
-    cols, att,
+    cols, q_out, peak_out, total_out, sum_out, keys, values,
     parts, hidden, cache, query, bias_ref, len_ref, mine, other,
     part_send, part_recv, send, one_y, one_x, all_y, all_x, hand, heard, load, pair_send, pair_recv,
 ):
@@ -125,22 +125,24 @@
     every = slice(None)
 
     def begin(stage):
-        first, n, _ = STAGES[stage]
+        first, n, part = STAGES[stage]
         pieces = [parts[p].astype(jnp.float32) for p in range(2 * first, 2 * (first + n))]
         cols[y, x, core, pl.ds(first * unit, n * unit), :] = jnp.concatenate(
             pieces, axis=0
         ).astype(jnp.bfloat16)
-        for d in reversed(ahead):
-            push(along_y(y, x, stage, core), replica(d, 0), 0, one_y.at[stage, y])
+        if part:
+            for d in reversed(ahead):
+                push(along_y(y, x, stage, core), replica(d, 0), 0, one_y.at[stage, y])
         for d in reversed(near):
             push(along_x(y, x, stage, core), replica(0, d), 0, one_x.at[stage, x])
 
     def turn(stage):
-        for d in ahead:
-            yy = wrap(y - d, NY)
-            arrived(along_y(yy, x, stage, core), one_y.at[stage, yy])
-        for d in reversed(near):
-            push(along_y(every, x, stage, core), replica(0, d), 1, all_x.at[stage, x])
+        if STAGES[stage][2]:
+            for d in ahead:
+                yy = wrap(y - d, NY)
+                arrived(along_y(yy, x, stage, core), one_y.at[stage, yy])
+            for d in reversed(near):
+                push(along_y(every, x, stage, core), replica(0, d), 1, all_x.at[stage, x])
         for d in near:
             xx = wrap(x - d, NX)
             arrived(along_x(y, xx, stage, core), one_x.at[stage, xx])
@@ -152,14 +154,16 @@
             yy = wrap(y - d, NY)
             arrived(along_x(yy, every, stage, core), all_y.at[stage, yy])
         push(along_x(every, every, stage, core), sibling, 3, hand.at[stage, 1])
-        for d in near:
-            xx = wrap(x - d, NX)
-            arrived(along_y(every, xx, stage, core), all_x.at[stage, xx])
-        push(along_y(every, every, stage, core), sibling, 3, hand.at[stage, 0])
+        if STAGES[stage][2]:
+            for d in near:
+                xx = wrap(x - d, NX)
+                arrived(along_y(every, xx, stage, core), all_x.at[stage, xx])
+            push(along_y(every, every, stage, core), sibling, 3, hand.at[stage, 0])
 
     def got(stage):
         arrived(along_x(every, every, stage, 1 - core), hand.at[stage, 1])
-        arrived(along_y(every, every, stage, 1 - core), hand.at[stage, 0])
+        if STAGES[stage][2]:
+            arrived(along_y(every, every, stage, 1 - core), hand.at[stage, 0])
 
     lane = lax.broadcasted_iota(jnp.int32, (1, HD), 1)
     half = lax.rem(lane, HD // 2).astype(jnp.float32)
@@ -175,7 +179,6 @@
     scale = 1.0 / math.sqrt(HD)
     n_att = query.shape[0]
     groups = query.shape[2] // HD
-    queries, peaks, totals, sums = [], [], [], []
 
     def attend_cached(i):
         if i == 0:
@@ -189,13 +192,13 @@
         s = jnp.where(place < len_ref[parity * n_att + i], s, NEG)
         m = jnp.max(s, axis=1, keepdims=True)
         e = jnp.exp(s - m)
-        queries.append(q)
-        peaks.append(m)
-        totals.append(jnp.sum(e, axis=1, keepdims=True))
-        sums.append(
-            jnp.dot(e.astype(jnp.bfloat16), cache[i, :, HD:], preferred_element_type=jnp.float32)
+        here = pl.ds(i * groups * STEPS, groups * STEPS)
+        q_out[here, :] = q
+        peak_out[here, :] = jnp.broadcast_to(m, q.shape)
+        total_out[here, :] = jnp.broadcast_to(jnp.sum(e, axis=1, keepdims=True), q.shape)
+        sum_out[here, :] = jnp.dot(
+            e.astype(jnp.bfloat16), cache[i, :, HD:], preferred_element_type=jnp.float32
         )
-
 
     def project(yy):
         wide = NX * 2 * block
@@ -235,62 +238,75 @@
             def _():
                 take(partner)
 
-    def hear(first):
-        for p in range(2 * first, NTEN, 2):
-
-            @pl.when(layer == 0)
-            def _():
-                take(p)
-                take(p + 1)
-                for r in plane:
-                    pl.semaphore_signal(
-                        heard.at[p // 2 - first], inc=1, device_id=(r, ten), device_id_type=MESH
-                    )
-
-            @pl.when(layer > 0)
-            def _():
-                take(p)
-                take(p + 1)
-                give(p)
-                give(p + 1)
-
-    def confirm(first):
-        for p in range(2 * first, NTEN, 2):
-
-            @pl.when(layer == 0)
-            def _():
-                pl.semaphore_wait(heard.at[p // 2 - first], len(plane))
-                give(p)
-                give(p + 1)
+    def hear():
+        for p in range(2 * LATE, NTEN):
+            take(p)
+
+    def tell():
+        for l in range(LATE, NTEN // 2):
+            for r in plane:
+                pl.semaphore_signal(
+                    heard.at[l - LATE], inc=1, device_id=(r, ten), device_id_type=MESH
+                )
+
+    def confirm():
+        for l in range(LATE, NTEN // 2):
+            pl.semaphore_wait(heard.at[l - LATE], len(plane))
+            give(2 * l)
+            give(2 * l + 1)
 
     loads[3].wait()
 
-    @pl.when(layer < 3)
+    @pl.when(layer == 0)
+    def _():
+        answer(0, 3)
+        meet(0, 3)
+        begin(0)
+        answer(3, 4)
+        begin(1)
+        turn(0)
+        answer(4, LATE)
+        hear()
+        begin(2)
+        tell()
+        turn(1)
+        turn(2)
+        confirm()
+        finish(0)
+        finish(1)
+        got(0)
+        got(1)
+        finish(2)
+        got(2)
+
+    @pl.when((layer > 0) & (layer < 3))
     def _():
         answer(0, 4)
         meet(0, 4)
-        begin(0)
-        answer(4, LATE)
-        hear(LATE)
-        begin(1)
-        turn(0)
-        confirm(LATE)
-        turn(1)
+        begin(3)
+        answer(4, 8)
+        begin(4)
+        turn(3)
+        turn(4)
+        finish(3)
+        got(3)
+        finish(4)
+        got(4)
 
     @pl.when(layer >= 3)
     def _():
         answer(3, 8)
         meet(0, 4)
-        begin(0)
+        begin(3)
         meet(4, 8)
-        begin(1)
-        turn(0)
-        turn(1)
-
-    finish(0)
-    got(0)
-    finish(1)
-    got(1)
+        begin(4)
+        turn(3)
+        turn(4)
+        finish(3)
+        got(3)
+        finish(4)
+        got(4)
+
     projected = project(0)
     for yy in range(1, NY):
         projected += project(yy)
@@ -308,30 +324,12 @@
     )
     exchange.start()
     exchange.wait()
-    kept, got = mine[parity], other[...]
-    new_keys = jnp.where(parity == 0, kept, got)
-    new_values = jnp.where(parity == 0, got, kept)
-
-    q = jnp.concatenate(queries, axis=0)
-    s = lax.dot_general(q, new_keys, NT, preferred_element_type=jnp.float32) * scale
-    of_query = lax.broadcasted_iota(jnp.int32, s.shape, 0)
-    of_key = lax.broadcasted_iota(jnp.int32, s.shape, 1)
-    same_row = lax.div(of_query, groups * STEPS) == lax.div(of_key, STEPS)
-    causal = lax.rem(of_key, STEPS) <= lax.rem(of_query, STEPS)
-    s = jnp.where(same_row & causal, s, NEG)
-    old_peak = jnp.concatenate(peaks, axis=0)
-    peak = jnp.maximum(old_peak, jnp.max(s, axis=1, keepdims=True))
-    e = jnp.exp(s - peak)
-    shrink = jnp.exp(old_peak - peak)
-    total = jnp.concatenate(totals, axis=0) * shrink + jnp.sum(e, axis=1, keepdims=True)
-    out = jnp.concatenate(sums, axis=0) * shrink
-    out += jnp.dot(e.astype(jnp.bfloat16), new_values, preferred_element_type=jnp.float32)
-    out = out / total
-    for i in range(n_att):
-        base = i * groups * STEPS
-        att[i] = jnp.concatenate(
-            [out[base + g * STEPS : base + (g + 1) * STEPS] for g in range(groups)], axis=1
-        ).astype(jnp.bfloat16)
+    kept, theirs = mine[parity], other[...]
+    new_keys = jnp.where(parity == 0, kept, theirs)
+    new_values = jnp.where(parity == 0, theirs, kept)
+
+    keys[...] = new_keys
+    values[...] = new_values
 
     given = parts.at[pl.ds(0, NTEN - 1)]
     pltpu.make_async_copy(given, given, part_send).wait()
@@ -346,6 +344,42 @@
         pltpu.make_async_copy(ref, ref, send.at[kind]).wait()
 
 
+def join(
+    STEPS,
+    cols, q_ref, peak_ref, total_ref, sum_ref, keys, values,
+    cols_out, att_out,
+    att, sems,
+):
+    out = pltpu.make_async_copy(cols, cols_out, sems.at[0])
+    out.start()
+    scale = 1.0 / math.sqrt(HD)
+    n_att, _, wide = att.shape
+    groups = wide // HD
+    s = lax.dot_general(q_ref[...], keys[...], NT, preferred_element_type=jnp.float32) * scale
+    of_query = lax.broadcasted_iota(jnp.int32, s.shape, 0)
+    of_key = lax.broadcasted_iota(jnp.int32, s.shape, 1)
+    same_row = lax.div(of_query, groups * STEPS) == lax.div(of_key, STEPS)
+    causal = lax.rem(of_key, STEPS) <= lax.rem(of_query, STEPS)
+    s = jnp.where(same_row & causal, s, NEG)
+    old_peak = peak_ref[...]
+    peak = jnp.maximum(old_peak, jnp.max(s, axis=1, keepdims=True))
+    e = jnp.exp(s - peak[:, : s.shape[1]])
+    shrink = jnp.exp(old_peak - peak)
+    total = total_ref[...] * shrink + jnp.sum(e, axis=1, keepdims=True)
+    mixed = sum_ref[...] * shrink
+    mixed += jnp.dot(e.astype(jnp.bfloat16), values[...], preferred_element_type=jnp.float32)
+    mixed = mixed / total
+    for i in range(n_att):
+        base = i * groups * STEPS
+        att[i] = jnp.concatenate(
+            [mixed[base + g * STEPS : base + (g + 1) * STEPS] for g in range(groups)], axis=1
+        ).astype(jnp.bfloat16)
+    done = pltpu.make_async_copy(att, att_out, sems.at[1])
+    done.start()
+    done.wait()
+    out.wait()
+
+
 def solution(mesh):
     n_rep, n_ten = mesh.shape["replica"], mesh.shape["tensor"]
     NX = 8
@@ -356,14 +390,19 @@
         piece = updated_rows.shape[0]
         vmem = pl.BlockSpec(memory_space=pltpu.VMEM)
         block = n_ten * piece
-        attended, columns = pl.pallas_call(
+        n_att, _, q_width = queries.shape[1:]
+        n_query = n_att * steps * (q_width // HD)
+        half = n_rows * steps // 2
+        gathered = pl.pallas_call(
             functools.partial(kernel, NY, NX, n_ten, piece, steps),
             out_shape=(
                 jax.ShapeDtypeStruct((NY, NX, 2, block, HD), jnp.bfloat16),
-                jax.ShapeDtypeStruct(queries.shape[1:], jnp.bfloat16),
+                jax.ShapeDtypeStruct((n_query, HD), jnp.bfloat16),
+                *[jax.ShapeDtypeStruct((n_query, HD), jnp.float32)] * 3,
+                *[jax.ShapeDtypeStruct((half, HD), jnp.bfloat16)] * 2,
             ),
             in_specs=[pl.BlockSpec(memory_space=pltpu.HBM)] * 6,
-            out_specs=(vmem, vmem),
+            out_specs=(vmem,) * 7,
             scratch_shapes=[
                 pltpu.VMEM((n_ten, piece, HD), jnp.bfloat16),
                 pltpu.VMEM((n_rows * steps, width), jnp.bfloat16),
@@ -397,7 +436,21 @@
                     cache_lengths,
                 )
             )
-        )[::-1]
+        )
+        columns, attended = pl.pallas_call(
+            functools.partial(join, steps),
+            out_shape=(
+                jax.ShapeDtypeStruct(gathered[0].shape, jnp.bfloat16),
+                jax.ShapeDtypeStruct(queries.shape[1:], jnp.bfloat16),
+            ),
+            in_specs=[pl.BlockSpec(memory_space=pl.ANY)] + [vmem] * 6,
+            out_specs=(pl.BlockSpec(memory_space=pltpu.HBM),) * 2,
+            scratch_shapes=[
+                pltpu.VMEM(queries.shape[1:], jnp.bfloat16),
+                pltpu.SemaphoreType.DMA((2,)),
+            ],
+            compiler_params=pltpu.CompilerParams(vmem_limit_bytes=16 << 20),
+        )(*gathered)
         return attended[None], columns.reshape(n_rep * block, HD)
 
     return jax.shard_map(

time: 48.4 us -> 51.9 us (1.072)
  the two profiles are of different devices: /device:TPU:1 before, /device:TPU:768 now
where the time goes in v4:
time: 51.9 us; the launch traced here: 51.7 us
  Pallas kernels  51.1 us (98%)
  between operations  0.64 us (1%)
    pallas_call x1, Pallas kernels, per_device(): pl.pallas_call(functools.partial(kernel, NY, NX, n_ten, piece, steps), ou...  49.7 us
    pallas_call x1, Pallas kernels, per_device(): pl.pallas_call(functools.partial(join, steps), out_shape=(jax.ShapeDtypeS...  1.34 us

profile of v4, /device:TPU:768, one launch (start us, length us, event | category | flops | bytes accessed | tf_op | source)
XLA Modules:
  0.0 51.7 jit_solution(10910660080827767343)
XLA Ops:
  0.6 49.7 %shard_map.77 = (bf16[4,8,2,128,128]{4,3,2,1,0:T(8,128)(2,1)S(1)}, bf16[256,128]{1,0:T(8,128)(2,1)S(1)}, f32[256,128]{1,0:T(8,128)S(1)}, f32[256,128]{1,0:T(8,12...) custom-call(bf16[8,2048]{1,0:T(8,128)(2,1)} %rows_hbm.1, ...), custom_call_target="tpu_custom_call" | custom-call | tf_op jit(solution)/shard_map/pallas_call | solution.py:396
  50.4 1.3 %shard_map.78 = (bf16[4,8,2,128,128]{4,3,2,1,0:T(8,128)(2,1)}, bf16[4,8,1024]{2,1,0:T(8,128)(2,1)}) custom-call(bf16[4,8,2,128,128]{4,3,2,1,0:T(8,128)(2,1)S(1)} %get-tuple-element.11.cols, bf16[256,128]{1,0:T(8,128)(2,1)S(1)} %get-tuple-element.12.q_ref, f32[256,128]{1,0:T(8,128)S(1)} %get-tuple-element.13.peak_ref, ...), custom_call_target="tpu_custom_call" | custom-call | tf_op jit(solution)/shard_map/pallas_call | solution.py:440

commit v5 on v4

--- a/solution.py
+++ b/solution.py
@@ -270,8 +270,8 @@
         begin(2)
         tell()
         turn(1)
+        confirm()
         turn(2)
-        confirm()
         finish(0)
         finish(1)
         got(0)

time: 51.9 us -> 46.7 us (0.90)
  the two profiles are of different devices: /device:TPU:768 before, /device:TPU:1 now
where the time goes in v5:
time: 46.7 us; the launch traced here: 46.6 us
  Pallas kernels  46 us (99%)
  between operations  0.64 us (1%)
    pallas_call x1, Pallas kernels, per_device(): pl.pallas_call(functools.partial(kernel, NY, NX, n_ten, piece, steps), ou...  44.6 us
    pallas_call x1, Pallas kernels, per_device(): pl.pallas_call(functools.partial(join, steps), out_shape=(jax.ShapeDtypeS...  1.34 us

profile of v5, /device:TPU:1, one launch (start us, length us, event | category | flops | bytes accessed | tf_op | source)
XLA Modules:
  0.0 46.6 jit_solution(12668884580918568591)
XLA Ops:
  0.6 44.6 %shard_map.77 = (bf16[4,8,2,128,128]{4,3,2,1,0:T(8,128)(2,1)S(1)}, bf16[256,128]{1,0:T(8,128)(2,1)S(1)}, f32[256,128]{1,0:T(8,128)S(1)}, f32[256,128]{1,0:T(8,12...) custom-call(bf16[8,2048]{1,0:T(8,128)(2,1)} %rows_hbm.1, ...), custom_call_target="tpu_custom_call" | custom-call | tf_op jit(solution)/shard_map/pallas_call | solution.py:396
  45.3 1.3 %shard_map.78 = (bf16[4,8,2,128,128]{4,3,2,1,0:T(8,128)(2,1)}, bf16[4,8,1024]{2,1,0:T(8,128)(2,1)}) custom-call(bf16[4,8,2,128,128]{4,3,2,1,0:T(8,128)(2,1)S(1)} %get-tuple-element.11.cols, bf16[256,128]{1,0:T(8,128)(2,1)S(1)} %get-tuple-element.12.q_ref, f32[256,128]{1,0:T(8,128)S(1)} %get-tuple-element.13.peak_ref, ...), custom_call_target="tpu_custom_call" | custom-call | tf_op jit(solution)/shard_map/pallas_call | solution.py:440

commit v6 on v5

--- a/solution.py
+++ b/solution.py
@@ -136,18 +136,24 @@
         for d in reversed(near):
             push(along_x(y, x, stage, core), replica(0, d), 0, one_x.at[stage, x])
 
-    def turn(stage):
+    def turn_y(stage):
         if STAGES[stage][2]:
             for d in ahead:
                 yy = wrap(y - d, NY)
                 arrived(along_y(yy, x, stage, core), one_y.at[stage, yy])
             for d in reversed(near):
                 push(along_y(every, x, stage, core), replica(0, d), 1, all_x.at[stage, x])
+
+    def turn_x(stage):
         for d in near:
             xx = wrap(x - d, NX)
             arrived(along_x(y, xx, stage, core), one_x.at[stage, xx])
         for d in reversed(ahead):
             push(along_x(y, every, stage, core), replica(d, 0), 2, all_y.at[stage, y])
+
+    def turn(stage):
+        turn_y(stage)
+        turn_x(stage)
 
     def finish(stage):
         for d in ahead:
@@ -270,8 +276,9 @@
         begin(2)
         tell()
         turn(1)
+        turn_y(2)
         confirm()
-        turn(2)
+        turn_x(2)
         finish(0)
         finish(1)
         got(0)

time: 46.7 us -> 47 us (level)
  no operation moved by 1% of the time
where the time goes in v6:
time: 47 us; the launch traced here: 46.8 us
  Pallas kernels  46.2 us (98%)
  between operations  0.64 us (1%)
    pallas_call x1, Pallas kernels, per_device(): pl.pallas_call(functools.partial(kernel, NY, NX, n_ten, piece, steps), ou...  44.9 us
    pallas_call x1, Pallas kernels, per_device(): pl.pallas_call(functools.partial(join, steps), out_shape=(jax.ShapeDtypeS...  1.34 us

profile of v6, /device:TPU:1, one launch (start us, length us, event | category | flops | bytes accessed | tf_op | source)
XLA Modules:
  0.0 46.8 jit_solution(16436518196684362806)
XLA Ops:
  0.6 44.9 %shard_map.77 = (bf16[4,8,2,128,128]{4,3,2,1,0:T(8,128)(2,1)S(1)}, bf16[256,128]{1,0:T(8,128)(2,1)S(1)}, f32[256,128]{1,0:T(8,128)S(1)}, f32[256,128]{1,0:T(8,12...) custom-call(bf16[8,2048]{1,0:T(8,128)(2,1)} %rows_hbm.1, ...), custom_call_target="tpu_custom_call" | custom-call | tf_op jit(solution)/shard_map/pallas_call | solution.py:403
  45.5 1.3 %shard_map.78 = (bf16[4,8,2,128,128]{4,3,2,1,0:T(8,128)(2,1)}, bf16[4,8,1024]{2,1,0:T(8,128)(2,1)}) custom-call(bf16[4,8,2,128,128]{4,3,2,1,0:T(8,128)(2,1)S(1)} %get-tuple-element.11.cols, bf16[256,128]{1,0:T(8,128)(2,1)S(1)} %get-tuple-element.12.q_ref, f32[256,128]{1,0:T(8,128)S(1)} %get-tuple-element.13.peak_ref, ...), custom_call_target="tpu_custom_call" | custom-call | tf_op jit(solution)/shard_map/pallas_call | solution.py:447
